TPU v7x, 512 devices: a whole 4x4x16 slice. The times are simulated.
512 devices in a mesh: gx: 4 (over z_lo), gy: 16 (over x, z_hi), gz: 8 (over y, core).
Axes of the slice: x: 4, y: 4, z: 16 (z_hi: 4, z_lo: 4; z = z_hi * 4 + z_lo), core: 2. Of those that a mesh axis runs over, the one named last changes fastest.
Arguments:
- e_field: float32 [3, 32, 128, 2048], P(None, 'gz', 'gx', 'gy'), may hold values from -6 to 6
- h_field: float32 [3, 32, 128, 2048], P(None, 'gz', 'gx', 'gy'), may hold values from -6 to 6
- pole_current: float32 [3, 32, 128, 2048], P(None, 'gz', 'gx', 'gy'), may hold values from -6 to 6
- material: int32 [32, 128, 2048], P('gz', 'gx', 'gy'), may hold values from 0 to 3
- pole_table: float32 [3, 4], replicated, may hold values from 0.2 to 0.9
- cotangent: float32 [16, 8, 4096], P(None, None, ('gx', 'gy', 'gz')), may hold values from -6 to 6
- cosines: float32 [2, 4096], P(None, ('gx', 'gy', 'gz')), may hold values from -0.7 to 0.7
- wavenumber: float32 [16], replicated, may hold values from 0.6 to 0.8
- time_phase: float32 [16], replicated, may hold values from -3.140625 to 3.140625
Outputs:
- e_next: float32 [3, 32, 128, 2048], P(None, 'gz', 'gx', 'gy')
- h_next: float32 [3, 32, 128, 2048], P(None, 'gz', 'gx', 'gy')
- pole_next: float32 [3, 32, 128, 2048], P(None, 'gz', 'gx', 'gy')
All inputs are finite; a program needn't handle non-finite values.
Results may differ from a plain program's by a relative error of at most 0.0003.
Values sent between devices are 32-bit elements; how exact they have to be, the bound alone decides.
A program may use at most 64 MiB of HBM per device.

v0:
```python
import math
import jax
import jax.numpy as jnp
from jax import lax
from jax.sharding import PartitionSpec as P

FREQS = 16
DIRS = 4096
NPOLE = 4
courant = 0.5


def turned_gather(arrays, axis, dims):
    turned = [jnp.moveaxis(a, dim, 0) for a, dim in zip(arrays, dims)]
    widths = [t[0].size for t in turned]
    both = jnp.concatenate([t.reshape(-1, w) for t, w in zip(turned, widths)], axis=1)
    filled = lax.all_gather(both, axis, axis=0, tiled=True)
    tiles = jnp.split(filled, [sum(widths[:k]) for k in range(1, len(widths))], axis=1)
    return tuple(
        (
            jnp.moveaxis(b.reshape(-1, *t.shape[1:]), 0, dim)
            for b, t, dim in zip(tiles, turned, dims)
        )
    )


def copy_for_each(array, axis):
    copies = jnp.broadcast_to(array, (lax.axis_size(axis), *array.shape))
    return lax.all_to_all(copies, axis, split_axis=0, concat_axis=0, tiled=True)


def of_everyone(array, axis):
    return copy_for_each(array, axis).sum(axis=0)


def from_behind(array, axis, by):
    size = lax.axis_size(axis)
    pairs = [(i, i + by) for i in range(size) if 0 <= i + by < size]
    return lax.ppermute(array, axis, pairs)


def surface_source(cotangent, cosines, wavenumber, time_phase, xs, ys):
    count = cotangent.shape[2]
    rows_x = xs.shape[0]
    rows_y = ys.shape[0]

    def one_freq(total, freq):
        wave = wavenumber[freq]
        along_x = wave * cosines[0]
        along_y = wave * cosines[1]
        phase_x = xs[:, None] * along_x[None, :] - time_phase[freq]
        phase_y = ys[:, None] * along_y[None, :]
        cos_x = jnp.cos(phase_x)[None]
        sin_x = jnp.sin(phase_x)[None]
        weights = cotangent[freq]
        real_part = weights[0::2][:, None, :]
        imag_part = weights[1::2][:, None, :]
        first = real_part * cos_x - imag_part * sin_x
        second = -(real_part * sin_x + imag_part * cos_x)
        left = jnp.concatenate([first, second], axis=2).reshape(4 * rows_x, 2 * count)
        right = jnp.concatenate([jnp.cos(phase_y), jnp.sin(phase_y)], axis=1).T
        part = jnp.dot(
            left, right, preferred_element_type=jnp.float32, precision=lax.Precision.HIGHEST
        )
        return (total + part.reshape(4, rows_x, rows_y), None)

    start = jnp.zeros((4, rows_x, rows_y), jnp.float32)
    total, _ = lax.scan(one_freq, start, jnp.arange(cotangent.shape[0], dtype=jnp.int32))
    return total


def ahead(value, nearby, axis):
    rest = lax.slice_in_dim(value, 1, value.shape[axis], axis=axis)
    return jnp.concatenate([rest, nearby], axis) - value


def behind(value, nearby, axis):
    rest = lax.slice_in_dim(value, 0, value.shape[axis] - 1, axis=axis)
    return value - jnp.concatenate([nearby, rest], axis)


def local(
    e_field, h_field, pole_current, material, pole_table, cotangent, cosines, wavenumber, time_phase
):
    depth, width_x, width_y = material.shape
    scale = 1.0 / math.sqrt(DIRS * FREQS)
    anchor_x = (lax.axis_index("gx") * width_x).astype(jnp.float32)
    anchor_y = (lax.axis_index("gy") * width_y).astype(jnp.float32)
    ys = anchor_y + jnp.arange(width_y).astype(jnp.float32)
    first_cot, first_cos = turned_gather((cotangent, cosines), "gx", (2, 1))
    band_cot, band_cos = turned_gather((first_cot, first_cos), "gy", (2, 1))
    xs = anchor_x + jnp.arange(width_x).astype(jnp.float32)
    partial_value = surface_source(band_cot, band_cos, wavenumber, time_phase, xs, ys)
    source = of_everyone(partial_value, "gz") * scale
    is_top = lax.axis_index("gz") == lax.axis_size("gz") - 1
    top = ((jnp.arange(depth) == depth - 1) & is_top).astype(jnp.float32)[:, None, None]
    next_x = from_behind(e_field[1:3, :, :1, :], "gx", -1)
    next_y = from_behind(e_field[0::2, :, :, :1], "gy", -1)
    next_z = from_behind(e_field[0:2, :1], "gz", -1)
    ex, ey, ez = (e_field[0], e_field[1], e_field[2])
    curl_x = ahead(ez, next_y[1], 2) - ahead(ey, next_z[1], 0)
    curl_y = ahead(ex, next_z[0], 0) - ahead(ez, next_x[1], 1)
    curl_z = ahead(ey, next_x[0], 1) - ahead(ex, next_y[0], 2)
    hx = h_field[0] - courant * curl_x - courant * top * source[2][None]
    hy = h_field[1] - courant * curl_y - courant * top * source[3][None]
    hz = h_field[2] - courant * curl_z
    h_next = jnp.stack([hx, hy, hz])
    prev_x = from_behind(h_next[1:3, :, -1:, :], "gx", 1)
    prev_y = from_behind(h_next[0::2, :, :, -1:], "gy", 1)
    prev_z = from_behind(h_next[0:2, -1:], "gz", 1)
    chosen = (material[None] == jnp.arange(NPOLE, dtype=jnp.int32)[:, None, None, None]).astype(
        jnp.float32
    )
    decay = jnp.sum(chosen * pole_table[0][:, None, None, None], axis=0)
    drive = jnp.sum(chosen * pole_table[1][:, None, None, None], axis=0)
    coef = jnp.sum(chosen * pole_table[2][:, None, None, None], axis=0)
    pole_next = decay[None] * pole_current + drive[None] * e_field
    side_x = behind(hz, prev_y[1], 2) - behind(hy, prev_z[1], 0)
    side_y = behind(hx, prev_z[0], 0) - behind(hz, prev_x[1], 1)
    side_z = behind(hy, prev_x[0], 1) - behind(hx, prev_y[0], 2)
    curl_h = jnp.stack([side_x, side_y, side_z])
    inject = jnp.stack([top * source[0][None], top * source[1][None], jnp.zeros_like(ex)])
    e_next = (
        e_field + coef[None] * (curl_h - 0.5 * (pole_next + pole_current)) - coef[None] * inject
    )
    return (e_next, h_next, pole_next)


def solution(mesh):
    in_specs = (
        P(None, "gz", "gx", "gy"),
        P(None, "gz", "gx", "gy"),
        P(None, "gz", "gx", "gy"),
        P("gz", "gx", "gy"),
        P(),
        P(None, None, ("gx", "gy", "gz")),
        P(None, ("gx", "gy", "gz")),
        P(),
        P(),
    )
    out_specs = (P(None, "gz", "gx", "gy"), P(None, "gz", "gx", "gy"), P(None, "gz", "gx", "gy"))
    return jax.shard_map(local, mesh=mesh, in_specs=in_specs, out_specs=out_specs, check_vma=False)
```

profile of v0, /device:TPU:11, one launch (start us, length us, event | category | flops | bytes accessed | tf_op | source)
XLA Modules:
  0.0 227.1 jit_solution(3024068051090232866)
XLA Ops:
  0.6 0.8 copy.38
  2.2 11.3 %all_gather.6 = f32[32,130]{1,0:T(8,128)S(1)} all-gather(f32[8,130]{1,0:T(8,128)S(1)} %pad_maximum_fusion.2), channel_id=1, replica_groups=mesh['gx'=4,'gy'=16,'gz'=8] {'gx'}, dimensions={0}, use_global_device_ids=true | all-gather | bytes 20800 | tf_op jit(solution)/shard_map/all_gather | solution.py:17
  13.6 52.0 %all_gather.7 = f32[512,130]{1,0:T(8,128)S(1)} all-gather(f32[32,130]{1,0:T(8,128)S(1)} %all_gather.6), channel_id=1, replica_groups=mesh['gx'=4,'gy'=16,'gz'=8] {'gy'}, dimensions={0}, use_global_device_ids=true | all-gather | bytes 282880 | tf_op jit(solution)/shard_map/all_gather | solution.py:17
  66.6 106.9 %while.11 = (s32[]{:T(128)}, f32[4,32,128]{2,1,0:T(8,128)S(1)}, s32[16]{0:T(128)S(1)}, f32[16,8,512]{2,1,0:T(8,128)S(1)}, f32[16]{0:T(128)S(1)}, /*index=5*/f32[...) while((s32[]{:T(128)}, f32[4,32,128]{2,1,0:T(8,128)S(1)}, ...), condition=%wide.region_2.3_spmd.clone, body=%wide.region_1.2_spmd.clone.sunk | while | flops 202179904 | bytes 2586073 | solution.py:68
  70.6 0.9 fusion.51
  71.6 1.0 multiply_cosine_fusion.2
  77.3 0.9 fusion.51
  78.3 1.0 multiply_cosine_fusion.2
  84.0 0.9 fusion.51
  85.0 1.0 multiply_cosine_fusion.2
  90.7 0.9 fusion.51
  91.7 1.0 multiply_cosine_fusion.2
  97.3 0.9 fusion.51
  98.4 1.0 multiply_cosine_fusion.2
  104.0 0.9 fusion.51
  105.0 1.0 multiply_cosine_fusion.2
  110.7 0.9 fusion.51
  111.7 1.0 multiply_cosine_fusion.2
  117.4 0.9 fusion.51
  118.4 1.0 multiply_cosine_fusion.2
  124.1 0.9 fusion.51
  125.1 1.0 multiply_cosine_fusion.2
  130.7 0.9 fusion.51
  131.8 1.0 multiply_cosine_fusion.2
  137.4 0.9 fusion.51
  138.5 1.0 multiply_cosine_fusion.2
  144.1 0.9 fusion.51
  145.1 1.0 multiply_cosine_fusion.2
  150.8 0.9 fusion.51
  151.8 1.0 multiply_cosine_fusion.2
  157.5 0.9 fusion.51
  158.5 1.0 multiply_cosine_fusion.2
  164.2 0.9 fusion.51
  165.2 1.0 multiply_cosine_fusion.2
  170.8 0.9 fusion.51
  171.9 1.0 multiply_cosine_fusion.2
  173.5 0.9 broadcast_in_dim.5
  174.3 15.4 %all-to-all-start = ((f32[8,4,32,128]{3,2,1,0:T(8,128)}), f32[8,4,32,128]{3,2,1,0:T(8,128)S(1)}, u32[]{:S(2)}, u32[]{:S(2)}) async-start(f32[8,4,32,128]{3,2,1,0:T(8,128)} %broadcast_in_dim.5), calls=%async_computation | async-start | bytes 1048576 | tf_op jit(solution)/shard_map/all_to_all | solution.py:29
  189.8 5.1 %collective-permute-start.1 = (f32[2,4,32,1]{3,2,1,0:T(8,128)S(1)}, f32[2,4,32,1]{3,2,1,0:T(8,128)S(1)}, u32[]{:S(2)}, u32[]{:S(2)}) collective-permute-start(f32[2,4,32,1]{3,2,1,0:T(8,128)S(1)} %slice.160), channel_id=1, source_target_pairs={{8,0},{16,8},{24,16},{32,24},{40,32},{48,40},{56,48},{64,56},{72,6... | collective-permute-start | bytes 3080 | tf_op jit(solution)/shard_map/ppermute | solution.py:39
  194.9 2.5 %collective-permute-start.2 = (f32[2,1,32,128]{3,2,1,0:T(8,128)S(1)}, f32[2,1,32,128]{3,2,1,0:T(8,128)S(1)}, u32[]{:S(2)}, u32[]{:S(2)}) collective-permute-start(f32[2,1,32,128]{3,2,1,0:T(8,128)S(1)} %slice.167), channel_id=1, source_target_pairs={{1,0},{2,1},{3,2},{4,3},{5,4},{6,5},{7,6},{9,8},{10,9},{11,10},{12... | collective-permute-start | bytes 98312 | tf_op jit(solution)/shard_map/ppermute | solution.py:39
  197.5 1.3 collective-permute-start
  200.0 6.9 %collective-permute-done.1 = f32[2,4,32,1]{3,2,1,0:T(8,128)S(1)} collective-permute-done((f32[2,4,32,1]{3,2,1,0:T(8,128)S(1)}, f32[2,4,32,1]{3,2,1,0:T(8,128)S(1)}, u32[]{:S(2)}, u32[]{:S(2)}) %collective-permute-start.1) | collective-permute-done | bytes 1056 | tf_op jit(solution)/shard_map/ppermute | solution.py:39
  207.1 0.9 copy-done.1
  209.1 2.3 %collective-permute-start.3 = (f32[2,4,32,1]{3,2,1,0:T(8,128)S(1)}, f32[2,4,32,1]{3,2,1,0:T(8,128)S(1)}, u32[]{:S(2)}, u32[]{:S(2)}) collective-permute-start(f32[2,4,32,1]{3,2,1,0:T(8,128)S(1)} %slice.176), channel_id=1, source_target_pairs={{0,8},{8,16},{16,24},{24,32},{32,40},{40,48},{48,56},{56,64},{64,7... | collective-permute-start | bytes 3080 | tf_op jit(solution)/shard_map/ppermute | solution.py:39
  211.4 1.3 collective-permute-start.5
  212.7 5.2 %collective-permute-start.4 = (f32[2,1,32,128]{3,2,1,0:T(8,128)S(1)}, f32[2,1,32,128]{3,2,1,0:T(8,128)S(1)}, u32[]{:S(2)}, u32[]{:S(2)}) collective-permute-start(f32[2,1,32,128]{3,2,1,0:T(8,128)S(1)} %pad_maximum_fusion.1), channel_id=1, source_target_pairs={{0,1},{1,2},{2,3},{3,4},{4,5},{5,6},{6,7},{8,9},{9,10},{10,11},{11... | collective-permute-start | bytes 98312 | tf_op jit(solution)/shard_map/ppermute | solution.py:39
  218.0 7.3 %collective-permute-done.3 = f32[2,4,32,1]{3,2,1,0:T(8,128)S(1)} collective-permute-done((f32[2,4,32,1]{3,2,1,0:T(8,128)S(1)}, f32[2,4,32,1]{3,2,1,0:T(8,128)S(1)}, u32[]{:S(2)}, u32[]{:S(2)}) %collective-permute-start.3) | collective-permute-done | bytes 1056 | tf_op jit(solution)/shard_map/ppermute | solution.py:39
  226.2 0.8 fusion.14
  (243 shorter events, 53.7 us)
Async XLA Ops:
  1.5 0.7 copy-start.6
  65.9 0.7 copy-start.7
  65.9 0.7 copy-start.8
  174.3 15.4 %copy-start = (f32[3,4,32,128]{3,2,1,0:T(8,128)S(1)}, f32[3,4,32,128]{3,2,1,0:T(8,128)}, u32[]{:S(2)}) copy-start(f32[3,4,32,128]{3,2,1,0:T(8,128)} %param.11) | copy-start | bytes 589828
  174.3 32.6 %all-to-all-start = ((f32[8,4,32,128]{3,2,1,0:T(8,128)}), f32[8,4,32,128]{3,2,1,0:T(8,128)S(1)}, u32[]{:S(2)}, u32[]{:S(2)}) async-start(f32[8,4,32,128]{3,2,1,0:T(8,128)} %broadcast_in_dim.5), calls=%async_computation | async-start | bytes 1048576 | tf_op jit(solution)/shard_map/all_to_all | solution.py:29
  189.8 17.1 %collective-permute-start.1 = (f32[2,4,32,1]{3,2,1,0:T(8,128)S(1)}, f32[2,4,32,1]{3,2,1,0:T(8,128)S(1)}, u32[]{:S(2)}, u32[]{:S(2)}) collective-permute-start(f32[2,4,32,1]{3,2,1,0:T(8,128)S(1)} %slice.160), channel_id=1, source_target_pairs={{8,0},{16,8},{24,16},{32,24},{40,32},{48,40},{56,48},{64,56},{72,6... | collective-permute-start | bytes 3080 | tf_op jit(solution)/shard_map/ppermute | solution.py:39
  194.9 12.0 %collective-permute-start.2 = (f32[2,1,32,128]{3,2,1,0:T(8,128)S(1)}, f32[2,1,32,128]{3,2,1,0:T(8,128)S(1)}, u32[]{:S(2)}, u32[]{:S(2)}) collective-permute-start(f32[2,1,32,128]{3,2,1,0:T(8,128)S(1)} %slice.167), channel_id=1, source_target_pairs={{1,0},{2,1},{3,2},{4,3},{5,4},{6,5},{7,6},{9,8},{10,9},{11,10},{12... | collective-permute-start | bytes 98312 | tf_op jit(solution)/shard_map/ppermute | solution.py:39
  197.5 9.5 %collective-permute-start = (f32[2,4,1,128]{3,2,1,0:T(1,128)S(1)}, f32[2,4,1,128]{3,2,1,0:T(1,128)S(1)}, u32[]{:S(2)}, u32[]{:S(2)}) collective-permute-start(f32[2,4,1,128]{3,2,1,0:T(1,128)S(1)} %slice.156), channel_id=1, source_target_pairs={{128,0},{256,128},{384,256},{129,1},{257,129},{385,257},{130,2},{2... | collective-permute-start | bytes 12296 | tf_op jit(solution)/shard_map/ppermute | solution.py:39
  198.9 0.8 copy-start.4
  198.9 0.7 copy-start.5
  207.0 0.9 copy-start.1
  208.3 0.7 copy-start.2
  209.1 16.2 %collective-permute-start.3 = (f32[2,4,32,1]{3,2,1,0:T(8,128)S(1)}, f32[2,4,32,1]{3,2,1,0:T(8,128)S(1)}, u32[]{:S(2)}, u32[]{:S(2)}) collective-permute-start(f32[2,4,32,1]{3,2,1,0:T(8,128)S(1)} %slice.176), channel_id=1, source_target_pairs={{0,8},{8,16},{16,24},{24,32},{32,40},{40,48},{48,56},{56,64},{64,7... | collective-permute-start | bytes 3080 | tf_op jit(solution)/shard_map/ppermute | solution.py:39
  211.4 13.9 %collective-permute-start.5 = (f32[2,4,1,128]{3,2,1,0:T(1,128)S(1)}, f32[2,4,1,128]{3,2,1,0:T(1,128)S(1)}, u32[]{:S(2)}, u32[]{:S(2)}) collective-permute-start(f32[2,4,1,128]{3,2,1,0:T(1,128)S(1)} %pad_maximum_fusion.3), channel_id=1, source_target_pairs={{0,128},{128,256},{256,384},{1,129},{129,257},{257,385},{2,130},{1... | collective-permute-start | bytes 12296 | tf_op jit(solution)/shard_map/ppermute | solution.py:39
  212.7 12.6 %collective-permute-start.4 = (f32[2,1,32,128]{3,2,1,0:T(8,128)S(1)}, f32[2,1,32,128]{3,2,1,0:T(8,128)S(1)}, u32[]{:S(2)}, u32[]{:S(2)}) collective-permute-start(f32[2,1,32,128]{3,2,1,0:T(8,128)S(1)} %pad_maximum_fusion.1), channel_id=1, source_target_pairs={{0,1},{1,2},{2,3},{3,4},{4,5},{5,6},{6,7},{8,9},{9,10},{10,11},{11... | collective-permute-start | bytes 98312 | tf_op jit(solution)/shard_map/ppermute | solution.py:39
  225.3 0.9 copy-start.3
where the time goes:
time: 228 us; the launch traced here: 227 us
  blocking collectives  63.3 us (28%)
  other arithmetic  41.8 us (18%)
  local copies, waits for them, and re-layouts  35.4 us (16%)
  starting transfers between devices  33.1 us (15%)
  loops' own time  28.5 us (12%)
  waiting for transfers between devices  14.2 us (6%)
  matrix products  9.66 us (4%)
    all_gather x2, blocking collectives, turned_gather(): filled = lax.all_gather(both, axis, axis=0, tiled=True)  63.3 us
    another operation x1, loops' own time, surface_source(): lax.scan(one_freq, start, jnp.arange(cotangent.shape[0], dtype=jnp.int32))  28.5 us
    ppermute x6, starting transfers between devices, from_behind(): return lax.ppermute(array, axis, pairs)  17.7 us
    cos x16, other arithmetic, one_freq(): right = jnp.concatenate([jnp.cos(phase_y), jnp.sin(phase_y)], axis=1).T  15.7 us
    all_to_all x1, starting transfers between devices, copy_for_each(): return lax.all_to_all(copies, axis, split_axis=0, concat_axis=0, tiled=True)  15.4 us
    ppermute x6, waiting for transfers between devices, from_behind(): return lax.ppermute(array, axis, pairs)  14.2 us
    cos x16, other arithmetic, one_freq(): cos_x = jnp.cos(phase_x)[None]  14 us
    dot_general x16, matrix products, one_freq(): jnp.dot(left, right, preferred_element_type=jnp.float32, precision=lax.Pr...  9.66 us
  transfers between devices with their start and end apart: 7, of which 2 were waited for; matrix products, arithmetic and copies ran while one was open for 0% of the time, Pallas kernels for 0%

commit v1 on v0

--- a/solution.py
+++ b/solution.py
@@ -14,7 +14,10 @@
     turned = [jnp.moveaxis(a, dim, 0) for a, dim in zip(arrays, dims)]
     widths = [t[0].size for t in turned]
     both = jnp.concatenate([t.reshape(-1, w) for t, w in zip(turned, widths)], axis=1)
-    filled = lax.all_gather(both, axis, axis=0, tiled=True)
+    devices = lax.axis_size(axis)
+    parts = jnp.stack([both for _ in range(devices)])
+    parts = lax.all_to_all(parts, axis, split_axis=0, concat_axis=0)
+    filled = jnp.concatenate(parts, axis=0)
     tiles = jnp.split(filled, [sum(widths[:k]) for k in range(1, len(widths))], axis=1)
     return tuple(
         (

time: 228 us -> 221 us (0.969)
  the two profiles are of different devices: /device:TPU:11 before, /device:TPU:3 now
where the time goes in v1:
time: 221 us; the launch traced here: 220 us
  waiting for transfers between devices  54.8 us (25%)
  other arithmetic  44.3 us (20%)
  starting transfers between devices  40.6 us (18%)
  local copies, waits for them, and re-layouts  37.2 us (17%)
  loops' own time  32.2 us (15%)
  matrix products  9.69 us (4%)
    all_to_all x2, waiting for transfers between devices, turned_gather(): parts = lax.all_to_all(parts, axis, split_axis=0, concat_axis=0)  33.5 us
    another operation x1, loops' own time, surface_source(): lax.scan(one_freq, start, jnp.arange(cotangent.shape[0], dtype=jnp.int32))  32.2 us
    ppermute x6, starting transfers between devices, from_behind(): return lax.ppermute(array, axis, pairs)  21.9 us
    cos x16, other arithmetic, one_freq(): right = jnp.concatenate([jnp.cos(phase_y), jnp.sin(phase_y)], axis=1).T  15.7 us
    cos x16, other arithmetic, one_freq(): cos_x = jnp.cos(phase_x)[None]  15.3 us
    all_to_all x2, starting transfers between devices, turned_gather(): parts = lax.all_to_all(parts, axis, split_axis=0, concat_axis=0)  13.7 us
    ppermute x6, waiting for transfers between devices, from_behind(): return lax.ppermute(array, axis, pairs)  11.9 us
    mul x16, other arithmetic, one_freq(): along_y = wave * cosines[1]  10.4 us
  transfers between devices with their start and end apart: 9, of which 3 were waited for; matrix products, arithmetic and copies ran while one was open for 38% of the time, Pallas kernels for 0%

profile of v1, /device:TPU:3, one launch (start us, length us, event | category | flops | bytes accessed | tf_op | source)
XLA Modules:
  0.0 219.9 jit_solution(6362701195088469926)
XLA Ops:
  0.6 0.9 copy.32
  3.0 5.6 %all-to-all-start = ((f32[4,8,130]{2,1,0:T(8,128)}), f32[4,8,130]{2,1,0:T(8,128)S(1)}, u32[]{:S(2)}, u32[]{:S(2)}) async-start(f32[4,8,130]{2,1,0:T(8,128)} %stack.16), calls=%async_computation | async-start | bytes 65536 | tf_op jit(solution)/shard_map/all_to_all | solution.py:19
  8.6 10.2 %collective-permute-start.1 = (f32[2,4,32,1]{3,2,1,0:T(8,128)S(1)}, f32[2,4,32,1]{3,2,1,0:T(8,128)S(1)}, u32[]{:S(2)}, u32[]{:S(2)}) collective-permute-start(f32[2,4,32,1]{3,2,1,0:T(8,128)S(1)} %slice.160), channel_id=1, source_target_pairs={{8,0},{16,8},{24,16},{32,24},{40,32},{48,40},{56,48},{64,56},{72,6... | collective-permute-start | bytes 3080 | tf_op jit(solution)/shard_map/ppermute | solution.py:42
  18.9 2.9 %collective-permute-start.2 = (f32[2,1,32,128]{3,2,1,0:T(8,128)S(1)}, f32[2,1,32,128]{3,2,1,0:T(8,128)S(1)}, u32[]{:S(2)}, u32[]{:S(2)}) collective-permute-start(f32[2,1,32,128]{3,2,1,0:T(8,128)S(1)} %slice.167), channel_id=1, source_target_pairs={{1,0},{2,1},{3,2},{4,3},{5,4},{6,5},{7,6},{9,8},{10,9},{11,10},{12... | collective-permute-start | bytes 98312 | tf_op jit(solution)/shard_map/ppermute | solution.py:42
  21.8 1.3 collective-permute-start
  24.9 8.1 %all-to-all-start.1 = ((f32[16,32,130]{2,1,0:T(8,128)}), f32[16,32,130]{2,1,0:T(8,128)S(1)}, u32[]{:S(2)}, u32[]{:S(2)}) async-start(f32[16,32,130]{2,1,0:T(8,128)} %stack.18), calls=%async_computation.1 | async-start | bytes 1048576 | tf_op jit(solution)/shard_map/all_to_all | solution.py:19
  33.1 33.5 %all-to-all-done.1 = f32[16,32,130]{2,1,0:T(8,128)S(1)} async-done(((f32[16,32,130]{2,1,0:T(8,128)}), f32[16,32,130]{2,1,0:T(8,128)S(1)}, u32[]{:S(2)}, u32[]{:S(2)}) %all-to-all-start.1) | async-done | bytes 266272 | tf_op jit(solution)/shard_map/all_to_all | solution.py:19
  67.6 113.6 %while.11 = (s32[]{:T(128)}, f32[4,32,128]{2,1,0:T(8,128)S(1)}, s32[16]{0:T(128)S(1)}, f32[16,8,512]{2,1,0:T(8,128)S(1)}, f32[16]{0:T(128)S(1)}, /*index=5*/f32[...) while((s32[]{:T(128)}, f32[4,32,128]{2,1,0:T(8,128)S(1)}, ...), condition=%wide.region_2.3_spmd.clone, body=%wide.region_1.2_spmd.clone.sunk | while | flops 202179904 | bytes 2586073 | solution.py:71
  72.0 1.0 fusion.51
  73.1 1.0 multiply_cosine_fusion.2
  79.1 1.0 fusion.51
  80.2 1.0 multiply_cosine_fusion.2
  86.2 1.0 fusion.51
  87.3 1.0 multiply_cosine_fusion.2
  93.3 1.0 fusion.51
  94.4 1.0 multiply_cosine_fusion.2
  100.4 1.0 fusion.51
  101.5 1.0 multiply_cosine_fusion.2
  107.5 1.0 fusion.51
  108.6 1.0 multiply_cosine_fusion.2
  114.6 1.0 fusion.51
  115.7 1.0 multiply_cosine_fusion.2
  121.7 1.0 fusion.51
  122.8 1.0 multiply_cosine_fusion.2
  128.8 1.0 fusion.51
  129.9 1.0 multiply_cosine_fusion.2
  135.9 1.0 fusion.51
  137.0 1.0 multiply_cosine_fusion.2
  143.0 1.0 fusion.51
  144.1 1.0 multiply_cosine_fusion.2
  150.1 1.0 fusion.51
  151.2 1.0 multiply_cosine_fusion.2
  157.2 1.0 fusion.51
  158.3 1.0 multiply_cosine_fusion.2
  164.3 1.0 fusion.51
  165.4 1.0 multiply_cosine_fusion.2
  171.4 1.0 fusion.51
  172.5 1.0 multiply_cosine_fusion.2
  178.5 1.0 fusion.51
  179.6 1.0 multiply_cosine_fusion.2
  181.2 0.8 broadcast_in_dim.5
  182.0 5.0 %all-to-all-start.2 = ((f32[8,4,32,128]{3,2,1,0:T(8,128)}), f32[8,4,32,128]{3,2,1,0:T(8,128)S(1)}, u32[]{:S(2)}, u32[]{:S(2)}) async-start(f32[8,4,32,128]{3,2,1,0:T(8,128)} %broadcast_in_dim.5), calls=%async_computation.2 | async-start | bytes 1048576 | tf_op jit(solution)/shard_map/all_to_all | solution.py:32
  187.1 9.4 %all-to-all-done.2 = f32[8,4,32,128]{3,2,1,0:T(8,128)S(1)} async-done(((f32[8,4,32,128]{3,2,1,0:T(8,128)}), f32[8,4,32,128]{3,2,1,0:T(8,128)S(1)}, u32[]{:S(2)}, u32[]{:S(2)}) %all-to-all-start.2) | async-done | bytes 524320 | tf_op jit(solution)/shard_map/all_to_all | solution.py:32
  196.6 0.9 copy-done.1
  198.6 1.9 collective-permute-start.3
  200.6 2.3 %collective-permute-start.5 = (f32[2,4,1,128]{3,2,1,0:T(1,128)S(1)}, f32[2,4,1,128]{3,2,1,0:T(1,128)S(1)}, u32[]{:S(2)}, u32[]{:S(2)}) collective-permute-start(f32[2,4,1,128]{3,2,1,0:T(1,128)S(1)} %pad_maximum_fusion.3), channel_id=1, source_target_pairs={{0,128},{128,256},{256,384},{1,129},{129,257},{257,385},{2,130},{1... | collective-permute-start | bytes 12296 | tf_op jit(solution)/shard_map/ppermute | solution.py:42
  202.9 3.3 %collective-permute-start.4 = (f32[2,1,32,128]{3,2,1,0:T(8,128)S(1)}, f32[2,1,32,128]{3,2,1,0:T(8,128)S(1)}, u32[]{:S(2)}, u32[]{:S(2)}) collective-permute-start(f32[2,1,32,128]{3,2,1,0:T(8,128)S(1)} %pad_maximum_fusion.1), channel_id=1, source_target_pairs={{0,1},{1,2},{2,3},{3,4},{4,5},{5,6},{6,7},{8,9},{9,10},{10,11},{11... | collective-permute-start | bytes 98312 | tf_op jit(solution)/shard_map/ppermute | solution.py:42
  206.2 11.8 %collective-permute-done.3 = f32[2,4,32,1]{3,2,1,0:T(8,128)S(1)} collective-permute-done((f32[2,4,32,1]{3,2,1,0:T(8,128)S(1)}, f32[2,4,32,1]{3,2,1,0:T(8,128)S(1)}, u32[]{:S(2)}, u32[]{:S(2)}) %collective-permute-start.3) | collective-permute-done | bytes 1056 | tf_op jit(solution)/shard_map/ppermute | solution.py:42
  (245 shorter events, 57.7 us)
Async XLA Ops:
  0.6 8.0 %copy-start = (f32[3,4,32,128]{3,2,1,0:T(8,128)S(1)}, f32[3,4,32,128]{3,2,1,0:T(8,128)}, u32[]{:S(2)}) copy-start(f32[3,4,32,128]{3,2,1,0:T(8,128)} %param.11) | copy-start | bytes 589828
  3.0 21.0 %all-to-all-start = ((f32[4,8,130]{2,1,0:T(8,128)}), f32[4,8,130]{2,1,0:T(8,128)S(1)}, u32[]{:S(2)}, u32[]{:S(2)}) async-start(f32[4,8,130]{2,1,0:T(8,128)} %stack.16), calls=%async_computation | async-start | bytes 65536 | tf_op jit(solution)/shard_map/all_to_all | solution.py:19
  8.6 15.1 %copy-start.4 = (s32[4,32,128]{2,1,0:T(8,128)S(1)}, s32[4,32,128]{2,1,0:T(8,128)}, u32[]{:S(2)}) copy-start(s32[4,32,128]{2,1,0:T(8,128)} %param.14) | copy-start | bytes 196612
  8.6 178.4 %collective-permute-start.1 = (f32[2,4,32,1]{3,2,1,0:T(8,128)S(1)}, f32[2,4,32,1]{3,2,1,0:T(8,128)S(1)}, u32[]{:S(2)}, u32[]{:S(2)}) collective-permute-start(f32[2,4,32,1]{3,2,1,0:T(8,128)S(1)} %slice.160), channel_id=1, source_target_pairs={{8,0},{16,8},{24,16},{32,24},{40,32},{48,40},{56,48},{64,56},{72,6... | collective-permute-start | bytes 3080 | tf_op jit(solution)/shard_map/ppermute | solution.py:42
  18.9 168.2 %collective-permute-start.2 = (f32[2,1,32,128]{3,2,1,0:T(8,128)S(1)}, f32[2,1,32,128]{3,2,1,0:T(8,128)S(1)}, u32[]{:S(2)}, u32[]{:S(2)}) collective-permute-start(f32[2,1,32,128]{3,2,1,0:T(8,128)S(1)} %slice.167), channel_id=1, source_target_pairs={{1,0},{2,1},{3,2},{4,3},{5,4},{6,5},{7,6},{9,8},{10,9},{11,10},{12... | collective-permute-start | bytes 98312 | tf_op jit(solution)/shard_map/ppermute | solution.py:42
  21.8 165.3 %collective-permute-start = (f32[2,4,1,128]{3,2,1,0:T(1,128)S(1)}, f32[2,4,1,128]{3,2,1,0:T(1,128)S(1)}, u32[]{:S(2)}, u32[]{:S(2)}) collective-permute-start(f32[2,4,1,128]{3,2,1,0:T(1,128)S(1)} %slice.156), channel_id=1, source_target_pairs={{128,0},{256,128},{384,256},{129,1},{257,129},{385,257},{130,2},{2... | collective-permute-start | bytes 12296 | tf_op jit(solution)/shard_map/ppermute | solution.py:42
  23.1 0.7 copy-start.5
  24.9 41.8 %all-to-all-start.1 = ((f32[16,32,130]{2,1,0:T(8,128)}), f32[16,32,130]{2,1,0:T(8,128)S(1)}, u32[]{:S(2)}, u32[]{:S(2)}) async-start(f32[16,32,130]{2,1,0:T(8,128)} %stack.18), calls=%async_computation.1 | async-start | bytes 1048576 | tf_op jit(solution)/shard_map/all_to_all | solution.py:19
  66.9 0.7 copy-start.6
  66.9 0.7 copy-start.7
  182.0 14.5 %all-to-all-start.2 = ((f32[8,4,32,128]{3,2,1,0:T(8,128)}), f32[8,4,32,128]{3,2,1,0:T(8,128)S(1)}, u32[]{:S(2)}, u32[]{:S(2)}) async-start(f32[8,4,32,128]{3,2,1,0:T(8,128)} %broadcast_in_dim.5), calls=%async_computation.2 | async-start | bytes 1048576 | tf_op jit(solution)/shard_map/all_to_all | solution.py:32
  196.6 0.9 copy-start.1
  197.8 0.7 copy-start.2
  198.6 19.4 %collective-permute-start.3 = (f32[2,4,32,1]{3,2,1,0:T(8,128)S(1)}, f32[2,4,32,1]{3,2,1,0:T(8,128)S(1)}, u32[]{:S(2)}, u32[]{:S(2)}) collective-permute-start(f32[2,4,32,1]{3,2,1,0:T(8,128)S(1)} %slice.176), channel_id=1, source_target_pairs={{0,8},{8,16},{16,24},{24,32},{32,40},{40,48},{48,56},{56,64},{64,7... | collective-permute-start | bytes 3080 | tf_op jit(solution)/shard_map/ppermute | solution.py:42
  200.6 17.5 %collective-permute-start.5 = (f32[2,4,1,128]{3,2,1,0:T(1,128)S(1)}, f32[2,4,1,128]{3,2,1,0:T(1,128)S(1)}, u32[]{:S(2)}, u32[]{:S(2)}) collective-permute-start(f32[2,4,1,128]{3,2,1,0:T(1,128)S(1)} %pad_maximum_fusion.3), channel_id=1, source_target_pairs={{0,128},{128,256},{256,384},{1,129},{129,257},{257,385},{2,130},{1... | collective-permute-start | bytes 12296 | tf_op jit(solution)/shard_map/ppermute | solution.py:42
  202.9 15.2 %collective-permute-start.4 = (f32[2,1,32,128]{3,2,1,0:T(8,128)S(1)}, f32[2,1,32,128]{3,2,1,0:T(8,128)S(1)}, u32[]{:S(2)}, u32[]{:S(2)}) collective-permute-start(f32[2,1,32,128]{3,2,1,0:T(8,128)S(1)} %pad_maximum_fusion.1), channel_id=1, source_target_pairs={{0,1},{1,2},{2,3},{3,4},{4,5},{5,6},{6,7},{8,9},{9,10},{10,11},{11... | collective-permute-start | bytes 98312 | tf_op jit(solution)/shard_map/ppermute | solution.py:42
  218.1 0.9 copy-start.3
